TPU v7x, 256 devices: a whole 4x4x8 slice. The times are simulated.
256 devices in a mesh: center: 64 (over y, z, core), rep: 4 (over x).
Axes of the slice: x: 4, y: 4, z: 8, core: 2. Of those that a mesh axis runs over, the one named last changes fastest.
Arguments:
- faces: bfloat16 [16384, 512], P(('center', 'rep')), may hold values from -1800 to 1800
- w_first: bfloat16 [512, 512], replicated, may hold values from -1.1 to 1.1
- w_second: bfloat16 [512, 512], replicated, may hold values from -1.1 to 1.1
- gain_first: float32 [512], replicated, may hold values from 0.46 to 1.54
- bias_first: float32 [512], replicated, may hold values from -3 to 3
- gain_second: float32 [512], replicated, may hold values from 0.46 to 1.54
- centers: float32 [131072, 512], P('center'), may hold values from -6 to 6
- momentum: float32 [131072, 512], P('center'), may hold values from -1.2 to 1.2
- sample_index: int32 [8192], P('center'), may hold values from 0 to 2047, as said below
- live_count: int32 [64], P('center'), may hold values from 16 to 128, as said below
- labels: int32 [16384], P(('center', 'rep')), may hold values from 0 to 8191, as said below
Outputs:
- loss: float32 [16384], P(('center', 'rep'))
- feat_grad: float32 [16384, 512], P(('center', 'rep'))
- new_centers: float32 [8192, 512], P('center')
- new_momentum: float32 [8192, 512], P('center')
Inputs may be any that keep to these rules, and one draw needn't show every extreme that they name: `sample_index`: the 128 entries of one shard are distinct rows of that shard. The live slots of a shard are its first live_count entries; some shard has 128 of them and some shard 128 // 8. `labels`: each label is a live sampled slot, counted over all shards' lists in shard order.
All inputs are finite; a program needn't handle non-finite values.
Results may differ from a plain program's by a relative error of at most 0.0075.
Values may be sent and summed in bfloat16 or wider, within the bound.
A program may use at most 64 MiB of HBM per device.

v0:
```python
import jax
import jax.numpy as jnp
from jax import lax
from jax.sharding import PartitionSpec as P

LOGIT_SCALE = 64.0
COS_MARGIN = 0.35
LEARN_RATE = 0.5
MOMENT_COEF = 0.9
DECAY_COEF = 0.0005
NORM_EPS = 1e-05
LENGTH_EPS = 1e-06


def batch_norm(values, gain_vec, sample_count):
    mean_vec = lax.psum(jnp.sum(values, 0), "rep") / sample_count
    centered = values - mean_vec
    spread = lax.psum(jnp.sum(centered * centered, 0), "rep") / sample_count
    return gain_vec * (values - mean_vec) * lax.rsqrt(spread + NORM_EPS)


def momentum_step(raw_grad, picked, center_len, center_unit, picked_momentum, live_slot):
    center_radial = jnp.sum(center_unit * raw_grad, 1, keepdims=True)
    center_grad = (raw_grad - center_unit * center_radial) / center_len
    velocity = MOMENT_COEF * picked_momentum + center_grad + DECAY_COEF * picked
    velocity = jnp.where(live_slot[:, None], velocity, picked_momentum)
    placed = jnp.where(live_slot[:, None], picked - LEARN_RATE * velocity, picked)
    return (placed, velocity)


def per_device(
    faces,
    w_first,
    w_second,
    gain_first,
    bias_first,
    gain_second,
    centers,
    momentum,
    sample_index,
    live_count,
    labels,
):
    face_rows = faces.shape[0]
    width = faces.shape[1]
    sample_count = face_rows * lax.axis_size("rep")
    first_out = jnp.dot(faces, w_first, preferred_element_type=jnp.float32)
    hidden = jnp.maximum(batch_norm(first_out, gain_first, sample_count) + bias_first, 0.0).astype(
        jnp.bfloat16
    )
    second = jnp.dot(hidden, w_second, preferred_element_type=jnp.float32)
    feature = batch_norm(second, gain_second, sample_count)
    length = jnp.sqrt(jnp.sum(feature * feature, 1, keepdims=True) + LENGTH_EPS)
    unit_rows = feature / length
    unit_low = unit_rows.astype(jnp.bfloat16)
    all_units, all_labels = (
        lax.all_gather(unit_low, "center", axis=0, tiled=True),
        lax.all_gather(labels, "center", axis=0, tiled=True),
    )
    my_shard = lax.axis_index("center")
    picked = jnp.take(centers, sample_index, axis=0)
    picked_momentum = jnp.take(momentum, sample_index, axis=0)
    center_len = jnp.sqrt(jnp.sum(picked * picked, 1, keepdims=True) + LENGTH_EPS)
    center_unit = picked / center_len
    center_low = center_unit.astype(jnp.bfloat16)
    slot_count = picked.shape[0]
    slot_ids = jnp.arange(slot_count, dtype=jnp.int32)
    live_slot = slot_ids < live_count[0]
    first_slot = my_shard * slot_count
    group_rows = all_units.shape[0]
    block_rows = min(1024, group_rows)
    block_total_count = group_rows // block_rows
    unit_blocks = all_units.reshape(block_total_count, block_rows, width)
    mark_blocks = all_labels.reshape(block_total_count, block_rows)

    def target_of(mark_block):
        return (mark_block - first_slot)[:, None] == slot_ids[None, :]

    def partials(element):
        cosine = jnp.einsum("fd,sd->fs", element[0], center_low, preferred_element_type=jnp.float32)
        target = target_of(element[1])
        logits = LOGIT_SCALE * (cosine - COS_MARGIN * target.astype(jnp.float32))
        exponent = jnp.where(live_slot[None, :], jnp.exp(logits), 0.0)
        return (exponent, jnp.sum(exponent, 1), jnp.sum(jnp.where(target, logits, 0.0), 1))

    exponent_blocks, local_total, local_target = lax.map(partials, (unit_blocks, mark_blocks))
    softmax_total, target_logit = lax.psum(
        (local_total.reshape(group_rows), local_target.reshape(group_rows)), "center"
    )
    group_loss = jnp.log(softmax_total) - target_logit
    loss = lax.dynamic_slice_in_dim(group_loss, my_shard * face_rows, face_rows, 0)
    total_blocks = softmax_total.reshape(block_total_count, block_rows)

    def grad_weight(exponent, mark_block, block_total):
        target = target_of(mark_block)
        return (
            LOGIT_SCALE * (exponent / block_total[:, None] - target.astype(jnp.float32))
        ).astype(jnp.bfloat16)

    start_sum = jnp.zeros((slot_count, width), jnp.float32)

    def both_block(running, element):
        weight = grad_weight(element[2], element[1], element[3])
        running = running + jnp.einsum(
            "fs,fd->sd", weight, element[0], preferred_element_type=jnp.float32
        )
        return (running, jnp.dot(weight, center_low, preferred_element_type=jnp.float32))

    center_raw, unit_terms = lax.scan(
        both_block, start_sum, (unit_blocks, mark_blocks, exponent_blocks, total_blocks)
    )
    unit_grad = lax.psum_scatter(
        unit_terms.reshape(group_rows, width), "center", scatter_dimension=0, tiled=True
    )
    radial = jnp.sum(unit_rows * unit_grad, 1, keepdims=True)
    feat_grad = (unit_grad - unit_rows * radial) / length
    raw_grad = lax.psum(center_raw, "rep")
    new_centers, new_momentum = momentum_step(
        raw_grad, picked, center_len, center_unit, picked_momentum, live_slot
    )
    return (loss, feat_grad, new_centers, new_momentum)


def solution(mesh):
    return jax.shard_map(
        per_device,
        mesh=mesh,
        in_specs=(
            P(("center", "rep"), None),
            P(),
            P(),
            P(),
            P(),
            P(),
            P("center", None),
            P("center", None),
            P("center"),
            P("center"),
            P(("center", "rep")),
        ),
        out_specs=(
            P(("center", "rep")),
            P(("center", "rep"), None),
            P("center", None),
            P("center", None),
        ),
        check_vma=False,
    )
```

profile of v0, /device:TPU:2, one launch (start us, length us, event | category | flops | bytes accessed | tf_op | source)
XLA Modules:
  0.0 792.8 jit_solution(13507264654186599052)
XLA Ops:
  9.3 10.0 %psum.49 = f32[512]{0:T(512)S(1)} all-reduce(f32[512]{0:T(512)S(1)} %get-tuple-element.251), channel_id=1, replica_groups=mesh['center'=64,'rep'=4] {'rep'}, use_global_device_ids=true, to_apply=%region_1.0 | all-reduce | flops 512 | bytes 4096 | tf_op jit(solution)/shard_map/psum | solution.py:16
  19.3 8.8 %psum.50 = f32[512]{0:T(512)S(1)} all-reduce(f32[512]{0:T(512)S(1)} %multiply_reduce_fusion.5), channel_id=1, replica_groups=mesh['center'=64,'rep'=4] {'rep'}, use_global_device_ids=true, to_apply=%region_3.0 | all-reduce | flops 512 | bytes 4096 | tf_op jit(solution)/shard_map/psum | solution.py:18
  29.4 8.7 %psum.51 = f32[512]{0:T(512)S(1)} all-reduce(f32[512]{0:T(512)S(1)} %get-tuple-element.253), channel_id=1, replica_groups=mesh['center'=64,'rep'=4] {'rep'}, use_global_device_ids=true, to_apply=%region_5.0 | all-reduce | flops 512 | bytes 4096 | tf_op jit(solution)/shard_map/psum | solution.py:16
  38.2 8.8 %psum.52 = f32[512]{0:T(512)S(1)} all-reduce(f32[512]{0:T(512)S(1)} %multiply_reduce_fusion.4), channel_id=1, replica_groups=mesh['center'=64,'rep'=4] {'rep'}, use_global_device_ids=true, to_apply=%region_7.0 | all-reduce | flops 512 | bytes 4096 | tf_op jit(solution)/shard_map/psum | solution.py:18
  52.1 249.9 %all-reduce = s32[4096]{0:T(1024)S(1)} all-reduce(s32[4096]{0:T(1024)S(1)} %dynamic-update-slice), channel_id=1, replica_groups=mesh['center'=64,'rep'=4] {'center'}, use_global_device_ids=true, to_apply=%add | all-reduce | flops 4096 | bytes 32768
  302.7 3.1 gather_fusion
  306.1 14.2 %while.29 = (s32[]{:T(128)}, f32[4,1024,128]{1,2,0:T(8,128)}, f32[4,1024]{1,0:T(4,128)S(1)}, f32[4,1024]{1,0:T(4,128)S(1)}, bf16[4,1024,512]{2,1,0:T(8,128)(2,1)...) while((s32[]{:T(128)}, f32[4,1024,128]{1,2,0:T(8,128)}, ...), condition=%wide.region_13.15_spmd.clone, body=%wide.region_10.14_spmd.clone.sunk | while | flops 135527552 | bytes 2795017 | solution.py:86
  306.8 2.6 bitcast_dynamic-update-slice_fusion.4
  310.4 2.6 bitcast_dynamic-update-slice_fusion.4
  314.0 2.5 bitcast_dynamic-update-slice_fusion.4
  317.5 2.5 bitcast_dynamic-update-slice_fusion.4
  320.3 246.2 %all-reduce.1 = (f32[4096]{0:T(1024)S(1)}, f32[4096]{0:T(1024)S(1)}) all-reduce(f32[4096]{0:T(1024)S(1)} %get-tuple-element.255, f32[4096]{0:T(1024)S(1)} %get-tuple-element.256), channel_id=1, replica_groups=mesh['center'=64,'rep'=4] {'center'}, use_global_device_ids=true, to_apply=%region_15.17 | all-reduce | flops 8192 | bytes 65536 | tf_op jit(solution)/shard_map/psum | solution.py:87
  566.5 20.6 %while.30 = (s32[]{:T(128)}, f32[128,512]{1,0:T(8,128)S(1)}, f32[4,1024,512]{2,1,0:T(8,128)}, f32[4,1024,128]{1,2,0:T(8,128)}, f32[4,1024]{1,0:T(4,128)S(1)}, /*...) while((s32[]{:T(128)}, f32[128,512]{1,0:T(8,128)S(1)}, ...), condition=%wide.region_17.19_spmd.clone.clone, body=%wide.region_16.18_spmd.clone.clone.sunk | while | flops 270140416 | bytes 6979735 | solution.py:109
  567.8 2.0 convolution_add_fusion.2
  569.8 1.9 bitcast_dynamic-update-slice_fusion.5
  573.0 2.0 convolution_add_fusion.2
  578.1 2.0 convolution_add_fusion.2
  580.1 1.8 bitcast_dynamic-update-slice_fusion.5
  583.3 2.0 convolution_add_fusion.2
  585.3 1.9 bitcast_dynamic-update-slice_fusion.5
  589.3 3.1 gather_fusion.1
  593.0 32.9 %all-reduce.4.cloned.1.call-done = f32[128,512]{1,0:T(8,128)} async-done(((f32[128,512]{1,0:T(8,128)}), f32[128,512]{1,0:T(8,128)}) %all-reduce.4.cloned.1.call-update) | async-done | bytes 262160 | tf_op jit(solution)/shard_map/psum | solution.py:117
  627.0 1.9 subtract_select_fusion
  628.9 154.6 %reduce-scatter.2.cloned.1.call-done = f32[64,512]{1,0:T(8,128)} async-done(((f32[4096,512]{1,0:T(8,128)}), f32[64,512]{1,0:T(8,128)}) %reduce-scatter.2.cloned.1.call-update) | async-done | bytes 131088 | tf_op jit(solution)/shard_map/reduce_scatter | solution.py:112
  (85 shorter events, 25.7 us)
Async XLA Ops:
  7.2 1.0 copy-start
  7.2 298.6 %copy-start.3 = (s32[128]{0:T(128)S(1)}, s32[128]{0:T(128)}, u32[]{:S(2)}) copy-start(s32[128]{0:T(128)} %param.25) | copy-start | bytes 1540
  7.2 298.9 %all-gather.2.cloned.1.call-start = ((), (), s32[]{:S(2)}) async-start(), calls=%async_computation.1 | async-start | bytes 4259840 | tf_op jit(solution)/shard_map/all_gather | solution.py:57
  49.2 576.6 %all-reduce.4.cloned.1.call-start = ((), (), s32[]{:S(2)}) async-start(), calls=%async_computation.3 | async-start | bytes 524288 | tf_op jit(solution)/shard_map/psum | solution.py:117
  587.1 0.7 copy-start.1
  587.8 195.6 %reduce-scatter.2.cloned.1.call-start = ((), (), s32[]{:S(2)}) async-start(), calls=%async_computation.2 | async-start | bytes 8519680 | tf_op jit(solution)/shard_map/reduce_scatter | solution.py:112
  588.6 194.9 %copy-start.2 = (f32[512]{0:T(512)S(1)}, f32[512]{0:T(512)}, u32[]{:S(2)}) copy-start(f32[512]{0:T(512)} %param.22) | copy-start | bytes 6148
Sparse Core Ops, SparseCore 0:
  49.3 80.5 all-gather.1
  588.0 37.8 all-reduce.3
  630.6 152.8 reduce-scatter.1
where the time goes:
time: 794 us; the launch traced here: 793 us
  blocking collectives  532 us (67%)
  waiting for transfers between devices  188 us (24%)
  matrix products  27.8 us (4%)
  local copies, waits for them, and re-layouts  15.7 us (2%)
  between operations  15.3 us (2%)
  other arithmetic  13.1 us (2%)
    unnamed x1, blocking collectives  250 us
    psum x1, blocking collectives, per_device(): lax.psum((local_total.reshape(group_rows), local_target.reshape(group_row...  246 us
    reduce_scatter x1, waiting for transfers between devices, per_device(): lax.psum_scatter(unit_terms.reshape(group_rows, width), 'center', scatter...  155 us
    psum x1, waiting for transfers between devices, per_device(): raw_grad = lax.psum(center_raw, 'rep')  32.9 us
    psum x2, blocking collectives, batch_norm(): mean_vec = lax.psum(jnp.sum(values, 0), 'rep') / sample_count  18.7 us
    psum x2, blocking collectives, batch_norm(): spread = lax.psum(jnp.sum(centered * centered, 0), 'rep') / sample_count  17.5 us
  transfers between devices with their start and end apart: 3, of which 2 were waited for; matrix products, arithmetic and copies ran while one was open for 2% of the time, Pallas kernels for 0%

commit v1 on v0

v1 whole, which is shorter than its diff:
```python
import jax
import jax.numpy as jnp
from jax import lax
from jax.experimental import pallas as pl
from jax.experimental.pallas import tpu as pltpu
from jax.sharding import PartitionSpec as P

LOGIT_SCALE = 64.0
COS_MARGIN = 0.35
LEARN_RATE = 0.5
MOMENT_COEF = 0.9
DECAY_COEF = 0.0005
NORM_EPS = 1e-05
LENGTH_EPS = 1e-06
DEAD_MARK = 2.0

D = 512
FACE = 64
SAMP = 128
ROWS = 2048
NY, NZ, NK, NX = 4, 8, 2, 4
QUART = SAMP // NX
GROUP = FACE * NX
BOTH = GROUP * NK
BLOCK = QUART * NY
SLOTS = BLOCK * NZ
MESH = pl.DeviceIdType.MESH
F32 = jnp.float32
BF16 = jnp.bfloat16

NEAR_FIRST = (1, 7, 2, 6, 3, 5, 4)
FAR_FIRST = (4, 3, 5, 2, 6, 1, 7, 0)
XK = tuple((dx, dk) for dk in range(NK) for dx in range(NX) if dx or dk)


def nt_dot(a, b):
    return lax.dot_general(a, b, (((1,), (1,)), ((), ())), preferred_element_type=F32)


def tn_dot(a, b):
    return lax.dot_general(a, b, (((0,), (0,)), ((), ())), preferred_element_type=F32)


def normalize(values, gain):
    mean = jnp.sum(values, 0, keepdims=True) * (1.0 / GROUP)
    centered = values - mean
    spread = jnp.sum(centered * centered, 0, keepdims=True) * (1.0 / GROUP)
    return centered * (gain * lax.rsqrt(spread + NORM_EPS))


def kernel(
    faces_ref, w_first_ref, w_second_ref, gain_first_ref, bias_first_ref, gain_second_ref,
    centers_ref, momentum_ref, labels_ref, index_ref, live_ref,
    loss_ref, feat_ref, new_centers_ref, new_momentum_ref,
    face_buf, w1_buf, w2_buf, table, mtable, label_send, label_buf, pick, mpick,
    low_all, unit_rows, inv_len, unit_all, expo, weight_all,
    sum_send, sum_buf, raw_own, raw_send, y_buf, z_send, z_buf, grad_send, grad_buf, x_buf,
    local_sem, face_ss, face_rs, label_ss, label_rs, low_ss, low_rs, unit_ss, unit_rs,
    sum_ss, sum_rs, y_ss, y_rs, z_ss, z_rs, grad_ss, grad_rs, x_ss, x_rs,
):
    c = lax.axis_index("center")
    x = lax.axis_index("rep")
    y = c // (NZ * NK)
    z = lax.rem(c // NK, NZ)
    k = lax.rem(c, NK)

    def device(dx=0, dy=0, dz=0, dk=0):
        yy = lax.rem(y + dy % NY, NY)
        zz = lax.rem(z + dz % NZ, NZ)
        kk = lax.rem(k + dk % NK, NK)
        return ((yy * NZ + zz) * NK + kk, lax.rem(x + dx % NX, NX))

    def send(src, dst, ss, rs, dev):
        copy = pltpu.make_async_remote_copy(
            src_ref=src, dst_ref=dst, send_sem=ss, recv_sem=rs, device_id=dev, device_id_type=MESH
        )
        copy.start()
        return copy

    table_copy = pltpu.make_async_copy(centers_ref, table, local_sem.at[0])
    table_copy.start()
    my_face = face_buf.at[pl.ds(pl.multiple_of(x * FACE, FACE), FACE)]
    face_copy = pltpu.make_async_copy(faces_ref, my_face, local_sem.at[1])
    face_copy.start()
    w1_copy = pltpu.make_async_copy(w_first_ref, w1_buf, local_sem.at[2])
    w1_copy.start()
    w2_copy = pltpu.make_async_copy(w_second_ref, w2_buf, local_sem.at[3])
    w2_copy.start()
    mtable_copy = pltpu.make_async_copy(momentum_ref, mtable, local_sem.at[4])
    mtable_copy.start()

    barrier = pltpu.get_barrier_semaphore()
    peers = [dict(dx=dx, dk=dk) for dx, dk in XK]
    peers += [dict(dy=dy) for dy in range(1, NY)]
    peers += [dict(dz=dz) for dz in range(1, NZ)]
    for peer in peers:
        pl.semaphore_signal(barrier, inc=1, device_id=device(**peer), device_id_type=MESH)

    label_send[...] = jnp.zeros_like(label_send)
    label_send[:, 0:FACE] = labels_ref[...]
    first_row = pl.multiple_of(x * QUART, QUART)
    table_copy.wait()

    def take_center(i, carry):
        for j in range(8):
            row = first_row + i * 8 + j
            pick[pl.ds(row, 1), :] = table[pl.ds(index_ref[row], 1), :]
        return carry

    lax.fori_loop(0, QUART // 8, take_center, 0)
    mine = pick[pl.ds(first_row, QUART), :]
    mine_len = jnp.sqrt(jnp.sum(mine * mine, 1, keepdims=True) + LENGTH_EPS)
    row_id = lax.broadcasted_iota(jnp.int32, (QUART, D), 0) + first_row
    col_id = lax.broadcasted_iota(jnp.int32, (QUART, D), 1)
    mark = jnp.where(col_id == 0, DEAD_MARK, 0.0)
    low_all[0:QUART, :] = jnp.where(row_id < live_ref[0], mine / mine_len, mark).astype(BF16)

    pl.semaphore_wait(barrier, len(peers))

    copies = []
    face_copies = [
        send(faces_ref, my_face, face_ss.at[dx - 1], face_rs.at[dx - 1], device(dx=dx))
        for dx in (1, 3, 2)
    ]
    low_copies = {}

    def low_block(dy, dz):
        return low_all.at[pl.ds((dz * NY + dy) * QUART, QUART)]

    def send_low(dz_from, dy, dz):
        at = dz * NY + dy
        low_copies[dy, dz] = send(
            low_block(0, dz_from), low_block(dy, dz), low_ss.at[at], low_rs.at[at],
            device(dy=dy, dz=dz - dz_from),
        )

    for dz in NEAR_FIRST:
        send_low(0, 0, dz)
    for dy in (1, 3, 2):
        send_low(0, dy, 0)
    label_copies = [
        send(label_send, label_buf.at[i], label_ss.at[i], label_rs.at[i], device(dx=dx, dk=dk))
        for i, (dx, dk) in enumerate(XK)
    ]

    def forward(dz):
        low_copies[0, dz].wait_recv()
        for dy in (1, 3, 2):
            send_low(dz, dy, dz)

    w1_copy.wait()
    face_copy.wait()
    for copy in face_copies:
        copy.wait_recv()
    first_out = jnp.dot(face_buf[...], w1_buf[...], preferred_element_type=F32)
    hidden = jnp.maximum(
        normalize(first_out, gain_first_ref[...]) + bias_first_ref[...], 0.0
    ).astype(BF16)
    forward(1)
    forward(7)
    w2_copy.wait()
    second = jnp.dot(hidden, w2_buf[...], preferred_element_type=F32)
    feature = normalize(second, gain_second_ref[...])
    length = jnp.sqrt(jnp.sum(feature * feature, 1, keepdims=True) + LENGTH_EPS)
    inverse = 1.0 / length
    inv_len[...] = inverse
    unit = feature * inverse
    unit_rows[...] = unit
    unit_all[0:GROUP, :] = unit.astype(BF16)
    unit_copy = send(
        unit_all.at[pl.ds(0, GROUP)], unit_all.at[pl.ds(GROUP, GROUP)],
        unit_ss, unit_rs, device(dk=1),
    )
    for dz in (2, 6, 3, 5, 4):
        forward(dz)

    for copy in label_copies:
        copy.wait_recv()
    label_parts = {(0, 0): label_send[0:1, 0:FACE]}
    for i, (dx, dk) in enumerate(XK):
        label_parts[dx, dk] = label_buf[i, 0:1, 0:FACE]
    halves = []
    for dk in range(NK):
        pieces = []
        for at in range(NX):
            piece = label_parts[0, dk]
            for dx in range(1, NX):
                piece = jnp.where(lax.rem(x - at + NX, NX) == dx, label_parts[dx, dk], piece)
            pieces.append(piece)
        halves.append(jnp.concatenate(pieces, 1))
    marks = jnp.concatenate(halves, 1)

    def block_rows(dz):
        return pl.ds(dz * BLOCK, BLOCK)

    in_block = lax.broadcasted_iota(jnp.int32, (QUART, 1), 0)

    def slot_ids(dz):
        parts = []
        for dy in range(NY):
            yy = lax.rem(y - dy + NY, NY)
            zz = lax.rem(z - dz + NZ, NZ)
            parts.append(in_block + (((yy * NZ + zz) * NK + k) * SAMP + first_row))
        return jnp.concatenate(parts, 0)

    unit_copy.wait_recv()
    totals = jnp.zeros((1, BOTH), F32)
    targets = jnp.zeros((1, BOTH), F32)
    for dz in (0,) + NEAR_FIRST:
        for dy in range(1, NY):
            low_copies[dy, dz].wait_recv()
        low = low_all[block_rows(dz), :]
        live = low[:, 0:128].astype(F32)[:, 0:1] < 0.75 * DEAD_MARK
        hit = slot_ids(dz) == marks
        cosine = nt_dot(low, unit_all[...])
        logits = LOGIT_SCALE * jnp.where(hit, cosine - COS_MARGIN, cosine)
        exponent = jnp.exp(jnp.where(live, logits, -1e30))
        expo[block_rows(dz), :] = exponent
        totals += jnp.sum(exponent, 0, keepdims=True)
        targets += jnp.sum(jnp.where(hit, logits, 0.0), 0, keepdims=True)
    sum_send[0:1, :] = totals
    sum_send[1:2, :] = targets
    sum_copies = [
        send(sum_send, sum_buf.at[i], sum_ss.at[i], sum_rs.at[i], device(dx=dx, dk=dk))
        for i, (dx, dk) in enumerate(XK)
    ]

    mtable_copy.wait()

    def take_rest(i, carry):
        for j in range(8):
            row = i * 8 + j
            at = index_ref[row]
            pick[pl.ds(row, 1), :] = table[pl.ds(at, 1), :]
            mpick[pl.ds(row, 1), :] = mtable[pl.ds(at, 1), :]
        return carry

    lax.fori_loop(0, SAMP // 8, take_rest, 0)

    sums = sum_send[...]
    for (dx, dk), i, copy in zip(XK, range(len(XK)), sum_copies):
        copy.wait_recv()
        part = sum_buf[i]
        if dk:
            part = jnp.concatenate([part[:, GROUP:], part[:, :GROUP]], 1)
        sums = sums + part
    inverse_total = 1.0 / sums[0:1, :]
    face_loss = jnp.log(sums[0:1, :GROUP]) - sums[1:2, :GROUP]
    my_loss = face_loss[:, 0:FACE]
    for at in range(1, NX):
        my_loss = jnp.where(x == at, face_loss[:, at * FACE : (at + 1) * FACE], my_loss)
    loss_ref[...] = my_loss

    y_copies = {}
    for dz in FAR_FIRST:
        hit = slot_ids(dz) == marks
        share = expo[block_rows(dz), :] * inverse_total
        weight = (LOGIT_SCALE * jnp.where(hit, share - 1.0, share)).astype(BF16)
        weight_all[block_rows(dz), :] = weight
        raw = jnp.dot(weight, unit_all[...], preferred_element_type=F32)
        raw_own[pl.ds(dz * QUART, QUART), :] = raw[0:QUART, :]
        raw_send[pl.ds(dz * (BLOCK - QUART), BLOCK - QUART), :] = raw[QUART:, :].astype(BF16)
        for dy in (2, 1, 3):
            at = dz * (NY - 1) + dy - 1
            y_copies[dy, dz] = send(
                raw_send.at[pl.ds(at * QUART, QUART)], y_buf.at[pl.ds(at * QUART, QUART)],
                y_ss.at[at], y_rs.at[at], device(dy=-dy),
            )

    grad = tn_dot(weight_all[...], low_all[...])
    grad_send[...] = grad.astype(BF16)
    grad_copies = []
    for i, (dx, dk) in enumerate(XK):
        there = dk * GROUP + lax.rem(x + dx, NX) * FACE
        grad_copies.append(
            send(
                grad_send.at[pl.ds(pl.multiple_of(there, FACE), FACE)], grad_buf.at[i],
                grad_ss.at[i], grad_rs.at[i], device(dx=dx, dk=dk),
            )
        )
    my_grad = grad[0:FACE, :]
    for at in range(1, NX):
        my_grad = jnp.where(x == at, grad[at * FACE : (at + 1) * FACE, :], my_grad)

    z_copies = []
    for dz in FAR_FIRST:
        total = raw_own[pl.ds(dz * QUART, QUART), :]
        for dy in range(1, NY):
            y_copies[dy, dz].wait_recv()
        for dy in range(1, NY):
            at = dz * (NY - 1) + dy - 1
            total = total + y_buf[pl.ds(at * QUART, QUART), :].astype(F32)
        if dz:
            z_send[dz - 1] = total.astype(BF16)
            z_copies.append(
                send(z_send.at[dz - 1], z_buf.at[dz - 1], z_ss.at[dz - 1], z_rs.at[dz - 1], device(dz=-dz))
            )
        else:
            raw_mine = total

    for i, copy in enumerate(grad_copies):
        copy.wait_recv()
        my_grad = my_grad + grad_buf[i].astype(F32)
    my_unit = unit_rows[pl.ds(pl.multiple_of(x * FACE, FACE), FACE), :]
    my_inverse = inv_len[pl.ds(pl.multiple_of(x * FACE, FACE), FACE), :]
    radial = jnp.sum(my_unit * my_grad, 1, keepdims=True)
    feat_ref[...] = (my_grad - my_unit * radial) * my_inverse

    for copy in z_copies:
        copy.wait_recv()
    for i in range(NZ - 1):
        raw_mine = raw_mine + z_buf[i].astype(F32)
    x_slot = x_buf.at[pl.ds(first_row, QUART)]
    x_buf[pl.ds(first_row, QUART), :] = raw_mine.astype(BF16)
    x_copies = [
        send(x_slot, x_slot, x_ss.at[dx - 1], x_rs.at[dx - 1], device(dx=dx)) for dx in (2, 1, 3)
    ]
    picked = pick[...]
    center_inv = 1.0 / jnp.sqrt(jnp.sum(picked * picked, 1, keepdims=True) + LENGTH_EPS)
    center_unit = picked * center_inv
    held = mpick[...]
    drift = MOMENT_COEF * held + DECAY_COEF * picked
    slot_live = lax.broadcasted_iota(jnp.int32, (SAMP, 1), 0) < live_ref[0]
    for copy in x_copies:
        copy.wait_recv()
    raw_grad = x_buf[...].astype(F32)
    center_radial = jnp.sum(center_unit * raw_grad, 1, keepdims=True)
    velocity = drift + (raw_grad - center_unit * center_radial) * center_inv
    velocity = jnp.where(slot_live, velocity, held)
    new_momentum_ref[...] = velocity
    new_centers_ref[...] = jnp.where(slot_live, picked - LEARN_RATE * velocity, picked)

    copies = face_copies + label_copies + list(low_copies.values()) + [unit_copy] + sum_copies
    copies += list(y_copies.values()) + grad_copies + z_copies + x_copies
    for copy in copies:
        copy.wait_send()


def per_device(
    faces, w_first, w_second, gain_first, bias_first, gain_second,
    centers, momentum, sample_index, live_count, labels,
):
    vmem = pl.BlockSpec(memory_space=pltpu.VMEM)
    smem = pl.BlockSpec(memory_space=pltpu.SMEM)
    hbm = pl.BlockSpec(memory_space=pl.ANY)
    dma = pltpu.SemaphoreType.DMA
    peers = len(XK)
    loss, feat, new_centers, new_momentum = pl.pallas_call(
        kernel,
        out_shape=(
            jax.ShapeDtypeStruct((1, FACE), F32),
            jax.ShapeDtypeStruct((FACE, D), F32),
            jax.ShapeDtypeStruct((SAMP, D), F32),
            jax.ShapeDtypeStruct((SAMP, D), F32),
        ),
        in_specs=[hbm, hbm, hbm, vmem, vmem, vmem, hbm, hbm, vmem, smem, smem],
        out_specs=(vmem, vmem, vmem, vmem),
        scratch_shapes=[
            pltpu.VMEM((GROUP, D), BF16),
            pltpu.VMEM((D, D), BF16),
            pltpu.VMEM((D, D), BF16),
            pltpu.VMEM((ROWS, D), F32),
            pltpu.VMEM((ROWS, D), F32),
            pltpu.VMEM((1, 128), jnp.int32),
            pltpu.VMEM((peers, 1, 128), jnp.int32),
            pltpu.VMEM((SAMP, D), F32),
            pltpu.VMEM((SAMP, D), F32),
            pltpu.VMEM((SLOTS, D), BF16),
            pltpu.VMEM((GROUP, D), F32),
            pltpu.VMEM((GROUP, 1), F32),
            pltpu.VMEM((BOTH, D), BF16),
            pltpu.VMEM((SLOTS, BOTH), F32),
            pltpu.VMEM((SLOTS, BOTH), BF16),
            pltpu.VMEM((2, BOTH), F32),
            pltpu.VMEM((peers, 2, BOTH), F32),
            pltpu.VMEM((NZ * QUART, D), F32),
            pltpu.VMEM((NZ * (NY - 1) * QUART, D), BF16),
            pltpu.VMEM((NZ * (NY - 1) * QUART, D), BF16),
            pltpu.VMEM((NZ - 1, QUART, D), BF16),
            pltpu.VMEM((NZ - 1, QUART, D), BF16),
            pltpu.VMEM((BOTH, D), BF16),
            pltpu.VMEM((peers, FACE, D), BF16),
            pltpu.VMEM((SAMP, D), BF16),
            dma((5,)),
            dma((NX - 1,)), dma((NX - 1,)),
            dma((peers,)), dma((peers,)),
            dma((NZ * NY,)), dma((NZ * NY,)),
            dma, dma,
            dma((peers,)), dma((peers,)),
            dma((NZ * (NY - 1),)), dma((NZ * (NY - 1),)),
            dma((NZ - 1,)), dma((NZ - 1,)),
            dma((peers,)), dma((peers,)),
            dma((NX - 1,)), dma((NX - 1,)),
        ],
        compiler_params=pltpu.CompilerParams(
            collective_id=1, has_side_effects=True, vmem_limit_bytes=48 * 2**20
        ),
        name="margin_step",
    )(
        faces, w_first, w_second, gain_first.reshape(1, D), bias_first.reshape(1, D),
        gain_second.reshape(1, D), centers, momentum, labels.reshape(1, FACE),
        sample_index, live_count,
    )
    return loss.reshape(FACE), feat, new_centers, new_momentum


def solution(mesh):
    return jax.shard_map(
        per_device,
        mesh=mesh,
        in_specs=(
            P(("center", "rep"), None),
            P(), P(), P(), P(), P(),
            P("center", None),
            P("center", None),
            P("center"),
            P("center"),
            P(("center", "rep")),
        ),
        out_specs=(
            P(("center", "rep")),
            P(("center", "rep"), None),
            P("center", None),
            P("center", None),
        ),
        check_vma=False,
    )
```

time: 794 us -> 65.4 us (0.08)
  blocking collectives: 532 us -> 0 us
  waiting for transfers between devices: 188 us -> 0 us
  Pallas kernels: 0 us -> 52.7 us
  matrix products: 27.8 us -> 0 us
  between operations: 15.3 us -> 1.31 us
  other arithmetic: 13.1 us -> 0 us
    psum x5 -> x0, blocking collectives: 282 us -> none  [the longest x1 246 us: per_device(): lax.psum((local_total.reshape(group_rows), local_target.reshape(group_row...]
    unnamed x1 -> x0, blocking collectives: 250 us -> none
    reduce_scatter x1 -> x0, waiting for transfers between devices: 155 us -> none  [per_device(): lax.psum_scatter(unit_terms.reshape(group_rows, width), 'center', scatter...]
    pallas_call x0 -> x1, Pallas kernels: none -> 52.7 us  [per_device(): pl.pallas_call(kernel, out_shape=(jax.ShapeDtypeStruct((1, FACE), F32), j...]
    psum x1 -> x0, waiting for transfers between devices: 32.9 us -> none  [per_device(): raw_grad = lax.psum(center_raw, 'rep')]
    dot_general x14 -> x0, matrix products: 27.8 us -> none  [the longest x4 10.2 us: partials(): jnp.einsum('fd,sd->fs', element[0], center_low, preferred_element_type=jn...]
  transfers between devices with their start and end apart: 3 -> 0, of which waited for: 2 -> 0; matrix products, arithmetic and copies ran while one was open for 2% -> 0% of each run, Pallas kernels for 0% -> 0%
where the time goes in v1:
time: 65.4 us; the launch traced here: 65 us
  Pallas kernels  52.7 us (81%)
  local copies, waits for them, and re-layouts  11 us (17%)
  between operations  1.31 us (2%)
    pallas_call x1, Pallas kernels, per_device(): pl.pallas_call(kernel, out_shape=(jax.ShapeDtypeStruct((1, FACE), F32), j...  52.7 us
    unnamed x22, local copies, waits for them, and re-layouts  11 us

profile of v1, /device:TPU:2, one launch (start us, length us, event | category | flops | bytes accessed | tf_op | source)
XLA Modules:
  0.0 65.0 jit_solution(7220056104122381466)
XLA Ops:
  1.3 0.0 copy-start
  1.3 2.2 %copy-done = f32[2048,512]{1,0:T(8,128)S(1)} copy-done((f32[2048,512]{1,0:T(8,128)S(1)}, f32[2048,512]{1,0:T(8,128)}, u32[]{:S(2)}) %copy-start) | copy-done | bytes 4194328
  3.5 0.0 copy-start.1
  3.5 1.0 %copy-done.1 = bf16[512,512]{1,0:T(8,128)(2,1)S(1)} copy-done((bf16[512,512]{1,0:T(8,128)(2,1)S(1)}, bf16[512,512]{1,0:T(8,128)(2,1)}, u32[]{:S(2)}) %copy-start.1) | copy-done | bytes 524312
  4.5 0.0 copy-start.2
  4.5 1.0 %copy-done.2 = bf16[512,512]{1,0:T(8,128)(2,1)S(1)} copy-done((bf16[512,512]{1,0:T(8,128)(2,1)S(1)}, bf16[512,512]{1,0:T(8,128)(2,1)}, u32[]{:S(2)}) %copy-start.2) | copy-done | bytes 524312
  5.6 0.0 copy-start.3
  5.6 0.8 %copy-done.3 = bf16[64,512]{1,0:T(8,128)(2,1)S(1)} copy-done((bf16[64,512]{1,0:T(8,128)(2,1)S(1)}, bf16[64,512]{1,0:T(8,128)(2,1)}, u32[]{:S(2)}) %copy-start.3) | copy-done | bytes 65560
  6.4 0.0 copy-start.4
  6.4 0.7 %copy-done.4 = f32[512]{0:T(512)S(1)} copy-done((f32[512]{0:T(512)S(1)}, f32[512]{0:T(512)}, u32[]{:S(2)}) %copy-start.4) | copy-done | bytes 2072
  7.1 0.0 copy-start.5
  7.1 0.7 %copy-done.5 = f32[512]{0:T(512)S(1)} copy-done((f32[512]{0:T(512)S(1)}, f32[512]{0:T(512)}, u32[]{:S(2)}) %copy-start.5) | copy-done | bytes 2072
  7.8 0.0 copy-start.6
  7.8 0.7 %copy-done.6 = f32[512]{0:T(512)S(1)} copy-done((f32[512]{0:T(512)S(1)}, f32[512]{0:T(512)}, u32[]{:S(2)}) %copy-start.6) | copy-done | bytes 2072
  8.4 0.0 copy-start.7
  8.4 0.7 %copy-done.7 = s32[64]{0:T(128)S(1)} copy-done((s32[64]{0:T(128)S(1)}, s32[64]{0:T(128)}, u32[]{:S(2)}) %copy-start.7) | copy-done | bytes 280
  9.1 0.0 copy-start.8
  9.1 0.7 %copy-done.8 = s32[128]{0:T(128)S(1)} copy-done((s32[128]{0:T(128)S(1)}, s32[128]{0:T(128)}, u32[]{:S(2)}) %copy-start.8) | copy-done | bytes 536
  9.8 52.7 %margin_step.1 = (f32[1,64]{1,0:T(1,128)S(1)}, f32[64,512]{1,0:T(8,128)S(1)}, f32[128,512]{1,0:T(8,128)S(1)}, f32[128,512]{1,0:T(8,128)S(1)}) custom-call(bf16[64,512]{1,0:T(8,128)(2,1)S(1)} %copy-done.3, bf16[512,512]{1,0:T(8,128)(2,1)S(1)} %copy-done.1, bf16[512,512]{1,0:T(8,128)(2,1)S(1)} %copy-done.2, f32[1,512]{1,0:T(1,128)S(1)} %bitcast.5, ...), custom_call_target="tpu_custom_call" | custom-call | tf_op jit(solution)/shard_map/margin_step/pallas_call | solution.py:348
  62.4 0.5 copy.20
  62.9 0.7 %copy.21 = f32[64,512]{1,0:T(8,128)} copy(f32[64,512]{1,0:T(8,128)S(1)} %get-tuple-element.17) | data formatting | bytes 262144
  63.6 0.7 %copy.22 = f32[128,512]{1,0:T(8,128)} copy(f32[128,512]{1,0:T(8,128)S(1)} %get-tuple-element.18) | data formatting | bytes 524288
  64.3 0.7 %copy.23 = f32[128,512]{1,0:T(8,128)} copy(f32[128,512]{1,0:T(8,128)S(1)} %get-tuple-element.19) | data formatting | bytes 524288
Async XLA Ops:
  1.3 2.2 %copy-start = (f32[2048,512]{1,0:T(8,128)S(1)}, f32[2048,512]{1,0:T(8,128)}, u32[]{:S(2)}) copy-start(f32[2048,512]{1,0:T(8,128)} %centers_ref.1) | copy-start | bytes 12582916
  3.5 1.0 %copy-start.1 = (bf16[512,512]{1,0:T(8,128)(2,1)S(1)}, bf16[512,512]{1,0:T(8,128)(2,1)}, u32[]{:S(2)}) copy-start(bf16[512,512]{1,0:T(8,128)(2,1)} %w_first_ref.1) | copy-start | bytes 1572868
  4.5 1.0 %copy-start.2 = (bf16[512,512]{1,0:T(8,128)(2,1)S(1)}, bf16[512,512]{1,0:T(8,128)(2,1)}, u32[]{:S(2)}) copy-start(bf16[512,512]{1,0:T(8,128)(2,1)} %w_second_ref.1) | copy-start | bytes 1572868
  5.6 0.8 %copy-start.3 = (bf16[64,512]{1,0:T(8,128)(2,1)S(1)}, bf16[64,512]{1,0:T(8,128)(2,1)}, u32[]{:S(2)}) copy-start(bf16[64,512]{1,0:T(8,128)(2,1)} %faces_ref.1) | copy-start | bytes 196612
  6.4 0.7 %copy-start.4 = (f32[512]{0:T(512)S(1)}, f32[512]{0:T(512)}, u32[]{:S(2)}) copy-start(f32[512]{0:T(512)} %param.14) | copy-start | bytes 6148
  7.1 0.7 %copy-start.5 = (f32[512]{0:T(512)S(1)}, f32[512]{0:T(512)}, u32[]{:S(2)}) copy-start(f32[512]{0:T(512)} %param.15) | copy-start | bytes 6148
  7.8 0.7 %copy-start.6 = (f32[512]{0:T(512)S(1)}, f32[512]{0:T(512)}, u32[]{:S(2)}) copy-start(f32[512]{0:T(512)} %param.16) | copy-start | bytes 6148
  8.4 0.7 %copy-start.7 = (s32[64]{0:T(128)S(1)}, s32[64]{0:T(128)}, u32[]{:S(2)}) copy-start(s32[64]{0:T(128)} %param.21) | copy-start | bytes 772
  9.1 0.7 %copy-start.8 = (s32[128]{0:T(128)S(1)}, s32[128]{0:T(128)}, u32[]{:S(2)}) copy-start(s32[128]{0:T(128)} %index_ref.1) | copy-start | bytes 1540

commit v2 on v1

--- a/solution.py
+++ b/solution.py
@@ -20,6 +20,7 @@
 ROWS = 2048
 NY, NZ, NK, NX = 4, 8, 2, 4
 QUART = SAMP // NX
+HALF = D // 2
 GROUP = FACE * NX
 BOTH = GROUP * NK
 BLOCK = QUART * NY
@@ -29,7 +30,10 @@
 BF16 = jnp.bfloat16
 
 NEAR_FIRST = (1, 7, 2, 6, 3, 5, 4)
-FAR_FIRST = (4, 3, 5, 2, 6, 1, 7, 0)
+ARRIVAL = (0,) + NEAR_FIRST
+BESIDE = (1, 7)
+BEYOND = (4, 3, 5, 2, 6)
+LAG = 3
 XK = tuple((dx, dk) for dk in range(NK) for dx in range(NX) if dx or dk)
 
 
@@ -49,14 +53,15 @@
 
 
 def kernel(
-    faces_ref, w_first_ref, w_second_ref, gain_first_ref, bias_first_ref, gain_second_ref,
-    centers_ref, momentum_ref, labels_ref, index_ref, live_ref,
+    faces_ref, w_first_ref, w_second_ref, gain_first_hbm, bias_first_hbm, gain_second_hbm,
+    centers_ref, momentum_ref, labels_hbm, index_hbm, live_ref,
     loss_ref, feat_ref, new_centers_ref, new_momentum_ref,
+    gain_first_ref, bias_first_ref, gain_second_ref, labels_ref, index_ref,
     face_buf, w1_buf, w2_buf, table, mtable, label_send, label_buf, pick, mpick,
     low_all, unit_rows, inv_len, unit_all, expo, weight_all,
-    sum_send, sum_buf, raw_own, raw_send, y_buf, z_send, z_buf, grad_send, grad_buf, x_buf,
-    local_sem, face_ss, face_rs, label_ss, label_rs, low_ss, low_rs, unit_ss, unit_rs,
-    sum_ss, sum_rs, y_ss, y_rs, z_ss, z_rs, grad_ss, grad_rs, x_ss, x_rs,
+    sum_send, sum_buf, raw_here, side_send, side_buf, row_send, row_buf, raw_own, raw_next, near_send, near_buf, far_send, far_buf, z_send, z_buf, grad_send, grad_buf, x_buf,
+    local_sem, face_ss, face_rs, label_ss, label_rs, low_ss, low_rs, half_ss, half_rs, unit_ss, unit_rs,
+    sum_ss, sum_rs, side_ss, side_rs, row_ss, row_rs, near_ss, near_rs, far_ss, far_rs, z_ss, z_rs, grad_ss, grad_rs, x_ss, x_rs,
 ):
     c = lax.axis_index("center")
     x = lax.axis_index("rep")
@@ -77,28 +82,35 @@
         copy.start()
         return copy
 
-    table_copy = pltpu.make_async_copy(centers_ref, table, local_sem.at[0])
-    table_copy.start()
     my_face = face_buf.at[pl.ds(pl.multiple_of(x * FACE, FACE), FACE)]
-    face_copy = pltpu.make_async_copy(faces_ref, my_face, local_sem.at[1])
-    face_copy.start()
-    w1_copy = pltpu.make_async_copy(w_first_ref, w1_buf, local_sem.at[2])
-    w1_copy.start()
-    w2_copy = pltpu.make_async_copy(w_second_ref, w2_buf, local_sem.at[3])
-    w2_copy.start()
-    mtable_copy = pltpu.make_async_copy(momentum_ref, mtable, local_sem.at[4])
-    mtable_copy.start()
+
+    def load(i, src, dst):
+        copy = pltpu.make_async_copy(src, dst, local_sem.at[i])
+        copy.start()
+        return copy
+
+    table_copy = load(0, centers_ref, table)
+    index_copy = load(1, index_hbm, index_ref)
 
     barrier = pltpu.get_barrier_semaphore()
-    peers = [dict(dx=dx, dk=dk) for dx, dk in XK]
-    peers += [dict(dy=dy) for dy in range(1, NY)]
-    peers += [dict(dz=dz) for dz in range(1, NZ)]
+    peers = [dict(dz=dz) for dz in reversed(NEAR_FIRST)]
+    peers += [dict(dx=dx, dk=dk) for dx, dk in XK]
+    peers += [dict(dy=dy) for dy in (2, 1, 3)]
     for peer in peers:
         pl.semaphore_signal(barrier, inc=1, device_id=device(**peer), device_id_type=MESH)
 
-    label_send[...] = jnp.zeros_like(label_send)
-    label_send[:, 0:FACE] = labels_ref[...]
+    label_copy = load(2, labels_hbm, labels_ref)
+    face_copy = load(3, faces_ref, my_face)
+    w1_copy = load(4, w_first_ref, w1_buf)
+    gain_copies = [
+        load(5, gain_first_hbm, gain_first_ref),
+        load(6, bias_first_hbm, bias_first_ref),
+        load(7, gain_second_hbm, gain_second_ref),
+    ]
+    w2_copy = load(8, w_second_ref, w2_buf)
     first_row = pl.multiple_of(x * QUART, QUART)
+
+    index_copy.wait()
     table_copy.wait()
 
     def take_center(i, carry):
@@ -117,37 +129,76 @@
 
     pl.semaphore_wait(barrier, len(peers))
 
-    copies = []
+    low_copies = {}
+
+    def low_block(dy, dz):
+        return low_all.at[pl.ds((dz * NY + dy) * QUART, QUART)]
+
+    def send_low(dz_from, dy, dz, dy_from=0):
+        at = dz * NY + dy
+        low_copies[dy, dz] = send(
+            low_block(dy_from, dz_from), low_block(dy, dz), low_ss.at[at], low_rs.at[at],
+            device(dy=dy - dy_from, dz=dz - dz_from),
+        )
+
+    def sideways(dy):
+        low_copies[dy, 0].wait_recv()
+        for dz in BESIDE:
+            send_low(0, dy, dz, dy)
+
+    half_copies = {}
+
+    def send_half(dz, part, dy_from):
+        low_copies[dy_from, dz].wait_recv()
+        rows = (dz * NY + dy_from) * QUART
+        there = (dz * NY + 2) * QUART
+        at = dz * 2 + part
+        half_copies[part, dz] = send(
+            low_all.at[pl.ds(rows, QUART), pl.ds(part * HALF, HALF)],
+            low_all.at[pl.ds(there, QUART), pl.ds(part * HALF, HALF)],
+            half_ss.at[at], half_rs.at[at], device(dy=dy_from),
+        )
+
+    def halves_on(dz):
+        send_half(dz, 0, 1)
+        send_half(dz, 1, NY - 1)
+
+    for dz in (2, 6):
+        send_low(0, 0, dz)
+    for dy in (1, 3):
+        send_low(0, dy, 0)
     face_copies = [
         send(faces_ref, my_face, face_ss.at[dx - 1], face_rs.at[dx - 1], device(dx=dx))
         for dx in (1, 3, 2)
     ]
-    low_copies = {}
-
-    def low_block(dy, dz):
-        return low_all.at[pl.ds((dz * NY + dy) * QUART, QUART)]
-
-    def send_low(dz_from, dy, dz):
-        at = dz * NY + dy
-        low_copies[dy, dz] = send(
-            low_block(0, dz_from), low_block(dy, dz), low_ss.at[at], low_rs.at[at],
-            device(dy=dy, dz=dz - dz_from),
-        )
-
-    for dz in NEAR_FIRST:
+    for dz in (3, 5, 4):
         send_low(0, 0, dz)
-    for dy in (1, 3, 2):
-        send_low(0, dy, 0)
+    send_low(0, 2, 0)
+    for dz in BESIDE:
+        send_low(0, 0, dz)
+
+    def forward(dz):
+        low_copies[0, dz].wait_recv()
+        for dy in (1, 3, 2) if dz == NZ // 2 else (1, 3):
+            send_low(dz, dy, dz)
+
+    sideways(1)
+    sideways(3)
+    forward(2)
+    forward(6)
+    sideways(2)
+    mtable_copy = load(9, momentum_ref, mtable)
+    label_copy.wait()
+    label_send[...] = jnp.zeros_like(label_send)
+    label_send[:, 0:FACE] = labels_ref[...]
     label_copies = [
         send(label_send, label_buf.at[i], label_ss.at[i], label_rs.at[i], device(dx=dx, dk=dk))
         for i, (dx, dk) in enumerate(XK)
     ]
 
-    def forward(dz):
-        low_copies[0, dz].wait_recv()
-        for dy in (1, 3, 2):
-            send_low(dz, dy, dz)
-
+
+    for copy in gain_copies:
+        copy.wait()
     w1_copy.wait()
     face_copy.wait()
     for copy in face_copies:
@@ -156,8 +207,8 @@
     hidden = jnp.maximum(
         normalize(first_out, gain_first_ref[...]) + bias_first_ref[...], 0.0
     ).astype(BF16)
-    forward(1)
-    forward(7)
+    for dz in (3, 5, 4):
+        forward(dz)
     w2_copy.wait()
     second = jnp.dot(hidden, w2_buf[...], preferred_element_type=F32)
     feature = normalize(second, gain_second_ref[...])
@@ -171,8 +222,8 @@
         unit_all.at[pl.ds(0, GROUP)], unit_all.at[pl.ds(GROUP, GROUP)],
         unit_ss, unit_rs, device(dk=1),
     )
-    for dz in (2, 6, 3, 5, 4):
-        forward(dz)
+    for dz in (2, 6, 3, 5):
+        halves_on(dz)
 
     for copy in label_copies:
         copy.wait_recv()
@@ -206,9 +257,18 @@
     unit_copy.wait_recv()
     totals = jnp.zeros((1, BOTH), F32)
     targets = jnp.zeros((1, BOTH), F32)
-    for dz in (0,) + NEAR_FIRST:
-        for dy in range(1, NY):
-            low_copies[dy, dz].wait_recv()
+    for step, dz in enumerate(ARRIVAL):
+        if dz == 0:
+            pass
+        elif dz in BESIDE:
+            for dy in range(NY):
+                low_copies[dy, dz].wait_recv()
+        elif dz == NZ // 2:
+            for dy in range(1, NY):
+                low_copies[dy, dz].wait_recv()
+        else:
+            for part in range(2):
+                half_copies[part, dz].wait_recv()
         low = low_all[block_rows(dz), :]
         live = low[:, 0:128].astype(F32)[:, 0:1] < 0.75 * DEAD_MARK
         hit = slot_ids(dz) == marks
@@ -225,18 +285,6 @@
         for i, (dx, dk) in enumerate(XK)
     ]
 
-    mtable_copy.wait()
-
-    def take_rest(i, carry):
-        for j in range(8):
-            row = i * 8 + j
-            at = index_ref[row]
-            pick[pl.ds(row, 1), :] = table[pl.ds(at, 1), :]
-            mpick[pl.ds(row, 1), :] = mtable[pl.ds(at, 1), :]
-        return carry
-
-    lax.fori_loop(0, SAMP // 8, take_rest, 0)
-
     sums = sum_send[...]
     for (dx, dk), i, copy in zip(XK, range(len(XK)), sum_copies):
         copy.wait_recv()
@@ -251,21 +299,64 @@
         my_loss = jnp.where(x == at, face_loss[:, at * FACE : (at + 1) * FACE], my_loss)
     loss_ref[...] = my_loss
 
-    y_copies = {}
-    for dz in FAR_FIRST:
+    def raw_grad_of(dz):
         hit = slot_ids(dz) == marks
         share = expo[block_rows(dz), :] * inverse_total
         weight = (LOGIT_SCALE * jnp.where(hit, share - 1.0, share)).astype(BF16)
         weight_all[block_rows(dz), :] = weight
-        raw = jnp.dot(weight, unit_all[...], preferred_element_type=F32)
-        raw_own[pl.ds(dz * QUART, QUART), :] = raw[0:QUART, :]
-        raw_send[pl.ds(dz * (BLOCK - QUART), BLOCK - QUART), :] = raw[QUART:, :].astype(BF16)
-        for dy in (2, 1, 3):
-            at = dz * (NY - 1) + dy - 1
-            y_copies[dy, dz] = send(
-                raw_send.at[pl.ds(at * QUART, QUART)], y_buf.at[pl.ds(at * QUART, QUART)],
-                y_ss.at[at], y_rs.at[at], device(dy=-dy),
+        return jnp.dot(weight, unit_all[...], preferred_element_type=F32)
+
+    side_copies = []
+    for i, dz in enumerate(BESIDE):
+        side_send[i] = raw_grad_of(dz).astype(BF16)
+        side_copies.append(
+            send(side_send.at[i], side_buf.at[i], side_ss.at[i], side_rs.at[i], device(dz=-dz))
+        )
+    near_copies = {}
+    for dz in BEYOND:
+        raw = raw_grad_of(dz)
+        part = [raw[dy * QUART : (dy + 1) * QUART, :] for dy in range(NY)]
+        keep = pl.ds(dz * QUART, QUART)
+        raw_own[keep, :] = part[0]
+        raw_next[keep, 0:HALF] = part[1][:, 0:HALF]
+        raw_next[keep, HALF:D] = part[3][:, HALF:D]
+        near_send[2 * dz, :, 0:HALF] = part[2][:, 0:HALF].astype(BF16)
+        near_send[2 * dz, :, HALF:D] = part[1][:, HALF:D].astype(BF16)
+        near_send[2 * dz + 1, :, 0:HALF] = part[3][:, 0:HALF].astype(BF16)
+        near_send[2 * dz + 1, :, HALF:D] = part[2][:, HALF:D].astype(BF16)
+        for way, dy in enumerate((-1, 1)):
+            at = 2 * dz + way
+            near_copies[way, dz] = send(
+                near_send.at[at], near_buf.at[at], near_ss.at[at], near_rs.at[at], device(dy=dy)
             )
+    raw_here[...] = raw_grad_of(0)
+
+    far_copies = {}
+    z_copies = []
+
+    def pass_on(dz):
+        for way, dy in enumerate((-1, 1)):
+            at = 2 * dz + way
+            columns = pl.ds(way * HALF, HALF)
+            near_copies[way, dz].wait_recv()
+            passed = raw_next[pl.ds(dz * QUART, QUART), columns] + near_buf[at, :, columns].astype(F32)
+            far_send[at] = passed.astype(BF16)
+            far_copies[way, dz] = send(
+                far_send.at[at], far_buf.at[at], far_ss.at[at], far_rs.at[at], device(dy=dy)
+            )
+
+    def gathered(dz):
+        for way in range(2):
+            far_copies[way, dz].wait_recv()
+        left = near_buf[2 * dz + 1, :, 0:HALF].astype(F32) + far_buf[2 * dz].astype(F32)
+        right = near_buf[2 * dz, :, HALF:D].astype(F32) + far_buf[2 * dz + 1].astype(F32)
+        return raw_own[pl.ds(dz * QUART, QUART), :] + jnp.concatenate([left, right], 1)
+
+    def send_on(dz):
+        z_send[dz - 1] = gathered(dz).astype(BF16)
+        z_copies.append(
+            send(z_send.at[dz - 1], z_buf.at[dz - 1], z_ss.at[dz - 1], z_rs.at[dz - 1], device(dz=-dz))
+        )
 
     grad = tn_dot(weight_all[...], low_all[...])
     grad_send[...] = grad.astype(BF16)
@@ -282,21 +373,42 @@
     for at in range(1, NX):
         my_grad = jnp.where(x == at, grad[at * FACE : (at + 1) * FACE, :], my_grad)
 
-    z_copies = []
-    for dz in FAR_FIRST:
-        total = raw_own[pl.ds(dz * QUART, QUART), :]
-        for dy in range(1, NY):
-            y_copies[dy, dz].wait_recv()
-        for dy in range(1, NY):
-            at = dz * (NY - 1) + dy - 1
-            total = total + y_buf[pl.ds(at * QUART, QUART), :].astype(F32)
-        if dz:
-            z_send[dz - 1] = total.astype(BF16)
-            z_copies.append(
-                send(z_send.at[dz - 1], z_buf.at[dz - 1], z_ss.at[dz - 1], z_rs.at[dz - 1], device(dz=-dz))
+    pass_on(BEYOND[0])
+    pass_on(BEYOND[1])
+    for copy in side_copies:
+        copy.wait_recv()
+    raw_mine = raw_here[0:QUART, :]
+    for i in range(2):
+        raw_mine = raw_mine + side_buf[i, 0:QUART, :].astype(F32)
+    rest = raw_here[QUART:BLOCK, :]
+    for i in range(2):
+        rest = rest + side_buf[i, QUART:BLOCK, :].astype(F32)
+    row_send[...] = rest.astype(BF16)
+    row_copies = []
+    for dy in (2, 1, 3):
+        row_copies.append(
+            send(
+                row_send.at[pl.ds((dy - 1) * QUART, QUART)], row_buf.at[pl.ds((dy - 1) * QUART, QUART)],
+                row_ss.at[dy - 1], row_rs.at[dy - 1], device(dy=-dy),
             )
-        else:
-            raw_mine = total
+        )
+    for step in range(2, len(BEYOND) + LAG):
+        if step < len(BEYOND):
+            pass_on(BEYOND[step])
+        if LAG <= step:
+            send_on(BEYOND[step - LAG])
+
+    mtable_copy.wait()
+
+    def take_rest(i, carry):
+        for j in range(8):
+            row = i * 8 + j
+            at = index_ref[row]
+            pick[pl.ds(row, 1), :] = table[pl.ds(at, 1), :]
+            mpick[pl.ds(row, 1), :] = mtable[pl.ds(at, 1), :]
+        return carry
+
+    lax.fori_loop(0, SAMP // 8, take_rest, 0)
 
     for i, copy in enumerate(grad_copies):
         copy.wait_recv()
@@ -306,10 +418,14 @@
     radial = jnp.sum(my_unit * my_grad, 1, keepdims=True)
     feat_ref[...] = (my_grad - my_unit * radial) * my_inverse
 
+    for copy in row_copies:
+        copy.wait_recv()
+    for i in range(NY - 1):
+        raw_mine = raw_mine + row_buf[pl.ds(i * QUART, QUART), :].astype(F32)
     for copy in z_copies:
         copy.wait_recv()
-    for i in range(NZ - 1):
-        raw_mine = raw_mine + z_buf[i].astype(F32)
+    for dz in BEYOND:
+        raw_mine = raw_mine + z_buf[dz - 1].astype(F32)
     x_slot = x_buf.at[pl.ds(first_row, QUART)]
     x_buf[pl.ds(first_row, QUART), :] = raw_mine.astype(BF16)
     x_copies = [
@@ -331,9 +447,20 @@
     new_centers_ref[...] = jnp.where(slot_live, picked - LEARN_RATE * velocity, picked)
 
     copies = face_copies + label_copies + list(low_copies.values()) + [unit_copy] + sum_copies
-    copies += list(y_copies.values()) + grad_copies + z_copies + x_copies
+    copies += list(half_copies.values()) + list(near_copies.values()) + list(far_copies.values())
+    copies += side_copies + row_copies
+    copies += grad_copies + z_copies + x_copies
     for copy in copies:
         copy.wait_send()
+
+
+def hand_over(*refs):
+    sems = refs[8]
+    copies = [pltpu.make_async_copy(refs[i], refs[i + 4], sems.at[i]) for i in range(4)]
+    for copy in copies:
+        copy.start()
+    for copy in copies:
+        copy.wait()
 
 
 def per_device(
@@ -342,10 +469,10 @@
 ):
     vmem = pl.BlockSpec(memory_space=pltpu.VMEM)
     smem = pl.BlockSpec(memory_space=pltpu.SMEM)
-    hbm = pl.BlockSpec(memory_space=pl.ANY)
+    hbm = pl.BlockSpec(memory_space=pltpu.HBM)
     dma = pltpu.SemaphoreType.DMA
     peers = len(XK)
-    loss, feat, new_centers, new_momentum = pl.pallas_call(
+    results = pl.pallas_call(
         kernel,
         out_shape=(
             jax.ShapeDtypeStruct((1, FACE), F32),
@@ -353,9 +480,14 @@
             jax.ShapeDtypeStruct((SAMP, D), F32),
             jax.ShapeDtypeStruct((SAMP, D), F32),
         ),
-        in_specs=[hbm, hbm, hbm, vmem, vmem, vmem, hbm, hbm, vmem, smem, smem],
+        in_specs=[hbm] * 10 + [smem],
         out_specs=(vmem, vmem, vmem, vmem),
         scratch_shapes=[
+            pltpu.VMEM((1, D), F32),
+            pltpu.VMEM((1, D), F32),
+            pltpu.VMEM((1, D), F32),
+            pltpu.VMEM((1, FACE), jnp.int32),
+            pltpu.SMEM((SAMP,), jnp.int32),
             pltpu.VMEM((GROUP, D), BF16),
             pltpu.VMEM((D, D), BF16),
             pltpu.VMEM((D, D), BF16),
@@ -373,21 +505,33 @@
             pltpu.VMEM((SLOTS, BOTH), BF16),
             pltpu.VMEM((2, BOTH), F32),
             pltpu.VMEM((peers, 2, BOTH), F32),
+            pltpu.VMEM((BLOCK, D), F32),
+            pltpu.VMEM((2, BLOCK, D), BF16),
+            pltpu.VMEM((2, BLOCK, D), BF16),
+            pltpu.VMEM((BLOCK - QUART, D), BF16),
+            pltpu.VMEM((BLOCK - QUART, D), BF16),
             pltpu.VMEM((NZ * QUART, D), F32),
-            pltpu.VMEM((NZ * (NY - 1) * QUART, D), BF16),
-            pltpu.VMEM((NZ * (NY - 1) * QUART, D), BF16),
+            pltpu.VMEM((NZ * QUART, D), F32),
+            pltpu.VMEM((2 * NZ, QUART, D), BF16),
+            pltpu.VMEM((2 * NZ, QUART, D), BF16),
+            pltpu.VMEM((2 * NZ, QUART, HALF), BF16),
+            pltpu.VMEM((2 * NZ, QUART, HALF), BF16),
             pltpu.VMEM((NZ - 1, QUART, D), BF16),
             pltpu.VMEM((NZ - 1, QUART, D), BF16),
             pltpu.VMEM((BOTH, D), BF16),
             pltpu.VMEM((peers, FACE, D), BF16),
             pltpu.VMEM((SAMP, D), BF16),
-            dma((5,)),
+            dma((10,)),
             dma((NX - 1,)), dma((NX - 1,)),
             dma((peers,)), dma((peers,)),
             dma((NZ * NY,)), dma((NZ * NY,)),
+            dma((2 * NZ,)), dma((2 * NZ,)),
             dma, dma,
             dma((peers,)), dma((peers,)),
-            dma((NZ * (NY - 1),)), dma((NZ * (NY - 1),)),
+            dma((2,)), dma((2,)),
+            dma((NY - 1,)), dma((NY - 1,)),
+            dma((2 * NZ,)), dma((2 * NZ,)),
+            dma((2 * NZ,)), dma((2 * NZ,)),
             dma((NZ - 1,)), dma((NZ - 1,)),
             dma((peers,)), dma((peers,)),
             dma((NX - 1,)), dma((NX - 1,)),
@@ -396,11 +540,20 @@
             collective_id=1, has_side_effects=True, vmem_limit_bytes=48 * 2**20
         ),
         name="margin_step",
-    )(
+    )(*[pltpu.with_memory_space_constraint(v, pltpu.HBM) for v in (
         faces, w_first, w_second, gain_first.reshape(1, D), bias_first.reshape(1, D),
         gain_second.reshape(1, D), centers, momentum, labels.reshape(1, FACE),
-        sample_index, live_count,
+        sample_index)], live_count,
     )
+    results = [pltpu.with_memory_space_constraint(r, pltpu.VMEM) for r in results]
+    loss, feat, new_centers, new_momentum = pl.pallas_call(
+        hand_over,
+        out_shape=tuple(jax.ShapeDtypeStruct(r.shape, r.dtype) for r in results),
+        in_specs=[pl.BlockSpec(memory_space=pltpu.VMEM)] * 4,
+        out_specs=(pl.BlockSpec(memory_space=pl.ANY),) * 4,
+        scratch_shapes=[dma((4,))],
+        name="hand_over",
+    )(*results)
     return loss.reshape(FACE), feat, new_centers, new_momentum
 
 

time: 65.4 us -> 52.1 us (0.80)
  local copies, waits for them, and re-layouts: 11 us -> 0 us
  Pallas kernels: 52.7 us -> 50.7 us
    unnamed x22 -> x0, local copies, waits for them, and re-layouts: 11 us -> none
    pallas_call x1, Pallas kernels: 52.7 us -> 49.8 us  [per_device(): pl.pallas_call(kernel, out_shape=(jax.ShapeDtypeStruct((1, FACE), F32), j...]
    pallas_call x0 -> x1, Pallas kernels: none -> 0.87 us  [per_device(): pl.pallas_call(hand_over, out_shape=tuple((jax.ShapeDtypeStruct(r.shape,...]
where the time goes in v2:
time: 52.1 us; the launch traced here: 52 us
  Pallas kernels  50.7 us (97%)
  between operations  1.29 us (2%)
    pallas_call x1, Pallas kernels, per_device(): pl.pallas_call(kernel, out_shape=(jax.ShapeDtypeStruct((1, FACE), F32), j...  49.8 us

profile of v2, /device:TPU:2, one launch (start us, length us, event | category | flops | bytes accessed | tf_op | source)
XLA Modules:
  0.0 52.0 jit_solution(10037775804393383277)
XLA Ops:
  1.3 49.8 %margin_step.1 = (f32[1,64]{1,0:T(1,128)S(1)}, f32[64,512]{1,0:T(8,128)S(1)}, f32[128,512]{1,0:T(8,128)S(1)}, f32[128,512]{1,0:T(8,128)S(1)}) custom-call(bf16[64,512]{1,0:T(8,128)(2,1)} %faces_ref.1, bf16[512,512]{1,0:T(8,128)(2,1)} %w_first_ref.1, bf16[512,512]{1,0:T(8,128)(2,1)} %w_second_ref.1, f32[1,512]{1,0:T(1,128)} %bitcast.5, f32[1,512]{1,0:T(1,128)} %bitcast.6, ...), custom_call_target="tpu_custom_call" | custom-call | tf_op jit(solution)/shard_map/margin_step/pallas_call | solution.py:475
  51.1 0.9 %hand_over.1 = (f32[1,64]{1,0:T(1,128)}, f32[64,512]{1,0:T(8,128)}, f32[128,512]{1,0:T(8,128)}, f32[128,512]{1,0:T(8,128)}) custom-call(f32[1,64]{1,0:T(1,128)S(1)} %get-tuple-element.12.refs_0_, f32[64,512]{1,0:T(8,128)S(1)} %get-tuple-element.13.refs_1_, f32[128,512]{1,0:T(8,128)S(1)} %get-tuple-element.14.refs_2_, f32[128,512]{1,0:T(8,128)S(1)} %get-tuple-element.15.refs_3_), custom_call_target="tpu_custom_call" | custom-call | tf_op jit(solution)/shard_map/hand_over/pallas_call | solution.py:549

commit v3 on v2

--- a/solution.py
+++ b/solution.py
@@ -18,9 +18,9 @@
 FACE = 64
 SAMP = 128
 ROWS = 2048
+PIECE = 512
 NY, NZ, NK, NX = 4, 8, 2, 4
 QUART = SAMP // NX
-HALF = D // 2
 GROUP = FACE * NX
 BOTH = GROUP * NK
 BLOCK = QUART * NY
@@ -33,7 +33,6 @@
 ARRIVAL = (0,) + NEAR_FIRST
 BESIDE = (1, 7)
 BEYOND = (4, 3, 5, 2, 6)
-LAG = 3
 XK = tuple((dx, dk) for dk in range(NK) for dx in range(NX) if dx or dk)
 
 
@@ -59,9 +58,9 @@
     gain_first_ref, bias_first_ref, gain_second_ref, labels_ref, index_ref,
     face_buf, w1_buf, w2_buf, table, mtable, label_send, label_buf, pick, mpick,
     low_all, unit_rows, inv_len, unit_all, expo, weight_all,
-    sum_send, sum_buf, raw_here, side_send, side_buf, row_send, row_buf, raw_own, raw_next, near_send, near_buf, far_send, far_buf, z_send, z_buf, grad_send, grad_buf, x_buf,
-    local_sem, face_ss, face_rs, label_ss, label_rs, low_ss, low_rs, half_ss, half_rs, unit_ss, unit_rs,
-    sum_ss, sum_rs, side_ss, side_rs, row_ss, row_rs, near_ss, near_rs, far_ss, far_rs, z_ss, z_rs, grad_ss, grad_rs, x_ss, x_rs,
+    sum_send, sum_buf, raw_here, side_send, side_buf, row_send, row_buf, raw_own, y_send, y_buf, z_send, z_buf, grad_send, grad_buf, x_buf,
+    local_sem, face_ss, face_rs, label_ss, label_rs, low_ss, low_rs, unit_ss, unit_rs,
+    sum_ss, sum_rs, side_ss, side_rs, row_ss, row_rs, y_ss, y_rs, z_ss, z_rs, grad_ss, grad_rs, x_ss, x_rs,
 ):
     c = lax.axis_index("center")
     x = lax.axis_index("rep")
@@ -89,7 +88,10 @@
         copy.start()
         return copy
 
-    table_copy = load(0, centers_ref, table)
+    table_copies = [
+        load(9 + i, centers_ref.at[pl.ds(i * PIECE, PIECE)], table.at[pl.ds(i * PIECE, PIECE)])
+        for i in range(ROWS // PIECE)
+    ]
     index_copy = load(1, index_hbm, index_ref)
 
     barrier = pltpu.get_barrier_semaphore()
@@ -111,7 +113,8 @@
     first_row = pl.multiple_of(x * QUART, QUART)
 
     index_copy.wait()
-    table_copy.wait()
+    for copy in table_copies:
+        copy.wait()
 
     def take_center(i, carry):
         for j in range(8):
@@ -145,23 +148,6 @@
         low_copies[dy, 0].wait_recv()
         for dz in BESIDE:
             send_low(0, dy, dz, dy)
-
-    half_copies = {}
-
-    def send_half(dz, part, dy_from):
-        low_copies[dy_from, dz].wait_recv()
-        rows = (dz * NY + dy_from) * QUART
-        there = (dz * NY + 2) * QUART
-        at = dz * 2 + part
-        half_copies[part, dz] = send(
-            low_all.at[pl.ds(rows, QUART), pl.ds(part * HALF, HALF)],
-            low_all.at[pl.ds(there, QUART), pl.ds(part * HALF, HALF)],
-            half_ss.at[at], half_rs.at[at], device(dy=dy_from),
-        )
-
-    def halves_on(dz):
-        send_half(dz, 0, 1)
-        send_half(dz, 1, NY - 1)
 
     for dz in (2, 6):
         send_low(0, 0, dz)
@@ -179,7 +165,7 @@
 
     def forward(dz):
         low_copies[0, dz].wait_recv()
-        for dy in (1, 3, 2) if dz == NZ // 2 else (1, 3):
+        for dy in (1, 3, 2):
             send_low(dz, dy, dz)
 
     sideways(1)
@@ -187,7 +173,7 @@
     forward(2)
     forward(6)
     sideways(2)
-    mtable_copy = load(9, momentum_ref, mtable)
+    mtable_copy = load(0, momentum_ref, mtable)
     label_copy.wait()
     label_send[...] = jnp.zeros_like(label_send)
     label_send[:, 0:FACE] = labels_ref[...]
@@ -222,9 +208,6 @@
         unit_all.at[pl.ds(0, GROUP)], unit_all.at[pl.ds(GROUP, GROUP)],
         unit_ss, unit_rs, device(dk=1),
     )
-    for dz in (2, 6, 3, 5):
-        halves_on(dz)
-
     for copy in label_copies:
         copy.wait_recv()
     label_parts = {(0, 0): label_send[0:1, 0:FACE]}
@@ -263,12 +246,9 @@
         elif dz in BESIDE:
             for dy in range(NY):
                 low_copies[dy, dz].wait_recv()
-        elif dz == NZ // 2:
+        else:
             for dy in range(1, NY):
                 low_copies[dy, dz].wait_recv()
-        else:
-            for part in range(2):
-                half_copies[part, dz].wait_recv()
         low = low_all[block_rows(dz), :]
         live = low[:, 0:128].astype(F32)[:, 0:1] < 0.75 * DEAD_MARK
         hit = slot_ids(dz) == marks
@@ -312,45 +292,29 @@
         side_copies.append(
             send(side_send.at[i], side_buf.at[i], side_ss.at[i], side_rs.at[i], device(dz=-dz))
         )
-    near_copies = {}
+    y_copies = {}
     for dz in BEYOND:
         raw = raw_grad_of(dz)
-        part = [raw[dy * QUART : (dy + 1) * QUART, :] for dy in range(NY)]
-        keep = pl.ds(dz * QUART, QUART)
-        raw_own[keep, :] = part[0]
-        raw_next[keep, 0:HALF] = part[1][:, 0:HALF]
-        raw_next[keep, HALF:D] = part[3][:, HALF:D]
-        near_send[2 * dz, :, 0:HALF] = part[2][:, 0:HALF].astype(BF16)
-        near_send[2 * dz, :, HALF:D] = part[1][:, HALF:D].astype(BF16)
-        near_send[2 * dz + 1, :, 0:HALF] = part[3][:, 0:HALF].astype(BF16)
-        near_send[2 * dz + 1, :, HALF:D] = part[2][:, HALF:D].astype(BF16)
-        for way, dy in enumerate((-1, 1)):
-            at = 2 * dz + way
-            near_copies[way, dz] = send(
-                near_send.at[at], near_buf.at[at], near_ss.at[at], near_rs.at[at], device(dy=dy)
+        raw_own[pl.ds(dz * QUART, QUART), :] = raw[0:QUART, :]
+        y_send[pl.ds(dz * (BLOCK - QUART), BLOCK - QUART), :] = raw[QUART:BLOCK, :].astype(BF16)
+        for dy in (2, 1, 3):
+            at = dz * (NY - 1) + dy - 1
+            y_copies[dy, dz] = send(
+                y_send.at[pl.ds(at * QUART, QUART)], y_buf.at[pl.ds(at * QUART, QUART)],
+                y_ss.at[at], y_rs.at[at], device(dy=-dy),
             )
     raw_here[...] = raw_grad_of(0)
 
-    far_copies = {}
     z_copies = []
 
-    def pass_on(dz):
-        for way, dy in enumerate((-1, 1)):
-            at = 2 * dz + way
-            columns = pl.ds(way * HALF, HALF)
-            near_copies[way, dz].wait_recv()
-            passed = raw_next[pl.ds(dz * QUART, QUART), columns] + near_buf[at, :, columns].astype(F32)
-            far_send[at] = passed.astype(BF16)
-            far_copies[way, dz] = send(
-                far_send.at[at], far_buf.at[at], far_ss.at[at], far_rs.at[at], device(dy=dy)
-            )
-
     def gathered(dz):
-        for way in range(2):
-            far_copies[way, dz].wait_recv()
-        left = near_buf[2 * dz + 1, :, 0:HALF].astype(F32) + far_buf[2 * dz].astype(F32)
-        right = near_buf[2 * dz, :, HALF:D].astype(F32) + far_buf[2 * dz + 1].astype(F32)
-        return raw_own[pl.ds(dz * QUART, QUART), :] + jnp.concatenate([left, right], 1)
+        total = raw_own[pl.ds(dz * QUART, QUART), :]
+        for dy in range(1, NY):
+            y_copies[dy, dz].wait_recv()
+        for dy in range(1, NY):
+            at = dz * (NY - 1) + dy - 1
+            total = total + y_buf[pl.ds(at * QUART, QUART), :].astype(F32)
+        return total
 
     def send_on(dz):
         z_send[dz - 1] = gathered(dz).astype(BF16)
@@ -373,8 +337,6 @@
     for at in range(1, NX):
         my_grad = jnp.where(x == at, grad[at * FACE : (at + 1) * FACE, :], my_grad)
 
-    pass_on(BEYOND[0])
-    pass_on(BEYOND[1])
     for copy in side_copies:
         copy.wait_recv()
     raw_mine = raw_here[0:QUART, :]
@@ -392,11 +354,8 @@
                 row_ss.at[dy - 1], row_rs.at[dy - 1], device(dy=-dy),
             )
         )
-    for step in range(2, len(BEYOND) + LAG):
-        if step < len(BEYOND):
-            pass_on(BEYOND[step])
-        if LAG <= step:
-            send_on(BEYOND[step - LAG])
+    for dz in BEYOND:
+        send_on(dz)
 
     mtable_copy.wait()
 
@@ -447,7 +406,7 @@
     new_centers_ref[...] = jnp.where(slot_live, picked - LEARN_RATE * velocity, picked)
 
     copies = face_copies + label_copies + list(low_copies.values()) + [unit_copy] + sum_copies
-    copies += list(half_copies.values()) + list(near_copies.values()) + list(far_copies.values())
+    copies += list(y_copies.values())
     copies += side_copies + row_copies
     copies += grad_copies + z_copies + x_copies
     for copy in copies:
@@ -511,27 +470,22 @@
             pltpu.VMEM((BLOCK - QUART, D), BF16),
             pltpu.VMEM((BLOCK - QUART, D), BF16),
             pltpu.VMEM((NZ * QUART, D), F32),
-            pltpu.VMEM((NZ * QUART, D), F32),
-            pltpu.VMEM((2 * NZ, QUART, D), BF16),
-            pltpu.VMEM((2 * NZ, QUART, D), BF16),
-            pltpu.VMEM((2 * NZ, QUART, HALF), BF16),
-            pltpu.VMEM((2 * NZ, QUART, HALF), BF16),
+            pltpu.VMEM((NZ * (NY - 1) * QUART, D), BF16),
+            pltpu.VMEM((NZ * (NY - 1) * QUART, D), BF16),
             pltpu.VMEM((NZ - 1, QUART, D), BF16),
             pltpu.VMEM((NZ - 1, QUART, D), BF16),
             pltpu.VMEM((BOTH, D), BF16),
             pltpu.VMEM((peers, FACE, D), BF16),
             pltpu.VMEM((SAMP, D), BF16),
-            dma((10,)),
+            dma((13,)),
             dma((NX - 1,)), dma((NX - 1,)),
             dma((peers,)), dma((peers,)),
             dma((NZ * NY,)), dma((NZ * NY,)),
-            dma((2 * NZ,)), dma((2 * NZ,)),
             dma, dma,
             dma((peers,)), dma((peers,)),
             dma((2,)), dma((2,)),
             dma((NY - 1,)), dma((NY - 1,)),
-            dma((2 * NZ,)), dma((2 * NZ,)),
-            dma((2 * NZ,)), dma((2 * NZ,)),
+            dma((NZ * (NY - 1),)), dma((NZ * (NY - 1),)),
             dma((NZ - 1,)), dma((NZ - 1,)),
             dma((peers,)), dma((peers,)),
             dma((NX - 1,)), dma((NX - 1,)),

time: 52.1 us -> 48.7 us (0.935)
  Pallas kernels: 50.7 us -> 47.4 us
    pallas_call x1, Pallas kernels: 49.8 us -> 46.5 us  [per_device(): pl.pallas_call(kernel, out_shape=(jax.ShapeDtypeStruct((1, FACE), F32), j...]
where the time goes in v3:
time: 48.7 us
  Pallas kernels  47.4 us (97%)
  between operations  1.29 us (3%)
    pallas_call x1, Pallas kernels, per_device(): pl.pallas_call(kernel, out_shape=(jax.ShapeDtypeStruct((1, FACE), F32), j...  46.5 us

profile of v3, /device:TPU:2, one launch (start us, length us, event | category | flops | bytes accessed | tf_op | source)
XLA Modules:
  0.0 48.7 jit_solution(3829262950383097774)
XLA Ops:
  1.3 46.5 %margin_step.1 = (f32[1,64]{1,0:T(1,128)S(1)}, f32[64,512]{1,0:T(8,128)S(1)}, f32[128,512]{1,0:T(8,128)S(1)}, f32[128,512]{1,0:T(8,128)S(1)}) custom-call(bf16[64,512]{1,0:T(8,128)(2,1)} %faces_ref.1, bf16[512,512]{1,0:T(8,128)(2,1)} %w_first_ref.1, bf16[512,512]{1,0:T(8,128)(2,1)} %w_second_ref.1, f32[1,512]{1,0:T(1,128)} %bitcast.5, f32[1,512]{1,0:T(1,128)} %bitcast.6, ...), custom_call_target="tpu_custom_call" | custom-call | tf_op jit(solution)/shard_map/margin_step/pallas_call | solution.py:434
  47.8 0.9 %hand_over.1 = (f32[1,64]{1,0:T(1,128)}, f32[64,512]{1,0:T(8,128)}, f32[128,512]{1,0:T(8,128)}, f32[128,512]{1,0:T(8,128)}) custom-call(f32[1,64]{1,0:T(1,128)S(1)} %get-tuple-element.12.refs_0_, f32[64,512]{1,0:T(8,128)S(1)} %get-tuple-element.13.refs_1_, f32[128,512]{1,0:T(8,128)S(1)} %get-tuple-element.14.refs_2_, f32[128,512]{1,0:T(8,128)S(1)} %get-tuple-element.15.refs_3_), custom_call_target="tpu_custom_call" | custom-call | tf_op jit(solution)/shard_map/hand_over/pallas_call | solution.py:503

commit v4 on v3

--- a/solution.py
+++ b/solution.py
@@ -30,7 +30,8 @@
 BF16 = jnp.bfloat16
 
 NEAR_FIRST = (1, 7, 2, 6, 3, 5, 4)
-ARRIVAL = (0,) + NEAR_FIRST
+EARLY = (0, 1, 7, 2, 6)
+LATE = (3, 5, 4)
 BESIDE = (1, 7)
 BEYOND = (4, 3, 5, 2, 6)
 XK = tuple((dx, dk) for dk in range(NK) for dx in range(NX) if dx or dk)
@@ -53,7 +54,7 @@
 
 def kernel(
     faces_ref, w_first_ref, w_second_ref, gain_first_hbm, bias_first_hbm, gain_second_hbm,
-    centers_ref, momentum_ref, labels_hbm, index_hbm, live_ref,
+    centers_ref, momentum_ref, labels_hbm, index_hbm, live_hbm,
     loss_ref, feat_ref, new_centers_ref, new_momentum_ref,
     gain_first_ref, bias_first_ref, gain_second_ref, labels_ref, index_ref,
     face_buf, w1_buf, w2_buf, table, mtable, label_send, label_buf, pick, mpick,
@@ -93,6 +94,7 @@
         for i in range(ROWS // PIECE)
     ]
     index_copy = load(1, index_hbm, index_ref)
+    live_ref = live_hbm
 
     barrier = pltpu.get_barrier_semaphore()
     peers = [dict(dz=dz) for dz in reversed(NEAR_FIRST)]
@@ -132,6 +134,10 @@
 
     pl.semaphore_wait(barrier, len(peers))
 
+    face_copies = [
+        send(faces_ref, my_face, face_ss.at[dx - 1], face_rs.at[dx - 1], device(dx=dx))
+        for dx in (1, 3, 2)
+    ]
     low_copies = {}
 
     def low_block(dy, dz):
@@ -153,10 +159,6 @@
         send_low(0, 0, dz)
     for dy in (1, 3):
         send_low(0, dy, 0)
-    face_copies = [
-        send(faces_ref, my_face, face_ss.at[dx - 1], face_rs.at[dx - 1], device(dx=dx))
-        for dx in (1, 3, 2)
-    ]
     for dz in (3, 5, 4):
         send_low(0, 0, dz)
     send_low(0, 2, 0)
@@ -193,7 +195,7 @@
     hidden = jnp.maximum(
         normalize(first_out, gain_first_ref[...]) + bias_first_ref[...], 0.0
     ).astype(BF16)
-    for dz in (3, 5, 4):
+    for dz in (3, 5):
         forward(dz)
     w2_copy.wait()
     second = jnp.dot(hidden, w2_buf[...], preferred_element_type=F32)
@@ -208,6 +210,7 @@
         unit_all.at[pl.ds(0, GROUP)], unit_all.at[pl.ds(GROUP, GROUP)],
         unit_ss, unit_rs, device(dk=1),
     )
+    forward(4)
     for copy in label_copies:
         copy.wait_recv()
     label_parts = {(0, 0): label_send[0:1, 0:FACE]}
@@ -237,27 +240,41 @@
             parts.append(in_block + (((yy * NZ + zz) * NK + k) * SAMP + first_row))
         return jnp.concatenate(parts, 0)
 
-    unit_copy.wait_recv()
-    totals = jnp.zeros((1, BOTH), F32)
-    targets = jnp.zeros((1, BOTH), F32)
-    for step, dz in enumerate(ARRIVAL):
-        if dz == 0:
-            pass
-        elif dz in BESIDE:
-            for dy in range(NY):
-                low_copies[dy, dz].wait_recv()
-        else:
-            for dy in range(1, NY):
-                low_copies[dy, dz].wait_recv()
+    def await_block(dz):
+        for dy in range(1 if dz not in BESIDE else 0, NY):
+            low_copies[dy, dz].wait_recv()
+
+    def score(dz, start, count):
+        faces_here = pl.ds(start, count)
         low = low_all[block_rows(dz), :]
         live = low[:, 0:128].astype(F32)[:, 0:1] < 0.75 * DEAD_MARK
-        hit = slot_ids(dz) == marks
-        cosine = nt_dot(low, unit_all[...])
+        hit = slot_ids(dz) == marks[:, start : start + count]
+        cosine = nt_dot(low, unit_all[faces_here, :])
         logits = LOGIT_SCALE * jnp.where(hit, cosine - COS_MARGIN, cosine)
         exponent = jnp.exp(jnp.where(live, logits, -1e30))
-        expo[block_rows(dz), :] = exponent
-        totals += jnp.sum(exponent, 0, keepdims=True)
-        targets += jnp.sum(jnp.where(hit, logits, 0.0), 0, keepdims=True)
+        expo[block_rows(dz), faces_here] = exponent
+        return (
+            jnp.sum(exponent, 0, keepdims=True),
+            jnp.sum(jnp.where(hit, logits, 0.0), 0, keepdims=True),
+        )
+
+    def add(a, b):
+        return a[0] + b[0], a[1] + b[1]
+
+    nothing = (jnp.zeros((1, GROUP), F32), jnp.zeros((1, GROUP), F32))
+    own, other = nothing, nothing
+    for dz in EARLY:
+        if dz:
+            await_block(dz)
+        own = add(own, score(dz, 0, GROUP))
+    unit_copy.wait_recv()
+    for dz in EARLY:
+        other = add(other, score(dz, GROUP, GROUP))
+    both = (jnp.concatenate([own[0], other[0]], 1), jnp.concatenate([own[1], other[1]], 1))
+    for dz in LATE:
+        await_block(dz)
+        both = add(both, score(dz, 0, BOTH))
+    totals, targets = both
     sum_send[0:1, :] = totals
     sum_send[1:2, :] = targets
     sum_copies = [
@@ -273,12 +290,6 @@
             part = jnp.concatenate([part[:, GROUP:], part[:, :GROUP]], 1)
         sums = sums + part
     inverse_total = 1.0 / sums[0:1, :]
-    face_loss = jnp.log(sums[0:1, :GROUP]) - sums[1:2, :GROUP]
-    my_loss = face_loss[:, 0:FACE]
-    for at in range(1, NX):
-        my_loss = jnp.where(x == at, face_loss[:, at * FACE : (at + 1) * FACE], my_loss)
-    loss_ref[...] = my_loss
-
     def raw_grad_of(dz):
         hit = slot_ids(dz) == marks
         share = expo[block_rows(dz), :] * inverse_total
@@ -304,6 +315,12 @@
                 y_ss.at[at], y_rs.at[at], device(dy=-dy),
             )
     raw_here[...] = raw_grad_of(0)
+
+    face_loss = jnp.log(sums[0:1, :GROUP]) - sums[1:2, :GROUP]
+    my_loss = face_loss[:, 0:FACE]
+    for at in range(1, NX):
+        my_loss = jnp.where(x == at, face_loss[:, at * FACE : (at + 1) * FACE], my_loss)
+    loss_ref[...] = my_loss
 
     z_copies = []
 
@@ -427,7 +444,6 @@
     centers, momentum, sample_index, live_count, labels,
 ):
     vmem = pl.BlockSpec(memory_space=pltpu.VMEM)
-    smem = pl.BlockSpec(memory_space=pltpu.SMEM)
     hbm = pl.BlockSpec(memory_space=pltpu.HBM)
     dma = pltpu.SemaphoreType.DMA
     peers = len(XK)
@@ -439,7 +455,7 @@
             jax.ShapeDtypeStruct((SAMP, D), F32),
             jax.ShapeDtypeStruct((SAMP, D), F32),
         ),
-        in_specs=[hbm] * 10 + [smem],
+        in_specs=[hbm] * 10 + [pl.BlockSpec(memory_space=pltpu.SMEM)],
         out_specs=(vmem, vmem, vmem, vmem),
         scratch_shapes=[
             pltpu.VMEM((1, D), F32),
@@ -477,7 +493,7 @@
             pltpu.VMEM((BOTH, D), BF16),
             pltpu.VMEM((peers, FACE, D), BF16),
             pltpu.VMEM((SAMP, D), BF16),
-            dma((13,)),
+            dma((14,)),
             dma((NX - 1,)), dma((NX - 1,)),
             dma((peers,)), dma((peers,)),
             dma((NZ * NY,)), dma((NZ * NY,)),

time: 48.7 us -> 48.5 us (level)
  no operation moved by 1% of the time
where the time goes in v4:
time: 48.5 us; the launch traced here: 48.4 us
  Pallas kernels  47.1 us (97%)
  between operations  1.29 us (3%)
    pallas_call x1, Pallas kernels, per_device(): pl.pallas_call(kernel, out_shape=(jax.ShapeDtypeStruct((1, FACE), F32), j...  46.2 us

profile of v4, /device:TPU:2, one launch (start us, length us, event | category | flops | bytes accessed | tf_op | source)
XLA Modules:
  0.0 48.4 jit_solution(5006155823437479627)
XLA Ops:
  1.3 46.2 %margin_step.1 = (f32[1,64]{1,0:T(1,128)S(1)}, f32[64,512]{1,0:T(8,128)S(1)}, f32[128,512]{1,0:T(8,128)S(1)}, f32[128,512]{1,0:T(8,128)S(1)}) custom-call(bf16[64,512]{1,0:T(8,128)(2,1)} %faces_ref.1, bf16[512,512]{1,0:T(8,128)(2,1)} %w_first_ref.1, bf16[512,512]{1,0:T(8,128)(2,1)} %w_second_ref.1, f32[1,512]{1,0:T(1,128)} %bitcast.5, f32[1,512]{1,0:T(1,128)} %bitcast.6, ...), custom_call_target="tpu_custom_call" | custom-call | tf_op jit(solution)/shard_map/margin_step/pallas_call | solution.py:450
  47.5 0.9 %hand_over.1 = (f32[1,64]{1,0:T(1,128)}, f32[64,512]{1,0:T(8,128)}, f32[128,512]{1,0:T(8,128)}, f32[128,512]{1,0:T(8,128)}) custom-call(f32[1,64]{1,0:T(1,128)S(1)} %get-tuple-element.12.refs_0_, f32[64,512]{1,0:T(8,128)S(1)} %get-tuple-element.13.refs_1_, f32[128,512]{1,0:T(8,128)S(1)} %get-tuple-element.14.refs_2_, f32[128,512]{1,0:T(8,128)S(1)} %get-tuple-element.15.refs_3_), custom_call_target="tpu_custom_call" | custom-call | tf_op jit(solution)/shard_map/hand_over/pallas_call | solution.py:519

commit v5 on v4

--- a/solution.py
+++ b/solution.py
@@ -167,7 +167,7 @@
 
     def forward(dz):
         low_copies[0, dz].wait_recv()
-        for dy in (1, 3, 2):
+        for dy in (2, 1, 3):
             send_low(dz, dy, dz)
 
     sideways(1)

time: 48.5 us -> 48.3 us (level)
  no operation moved by 1% of the time
where the time goes in v5:
time: 48.3 us; the launch traced here: 48.1 us
  Pallas kernels  46.8 us (97%)
  between operations  1.29 us (3%)
    pallas_call x1, Pallas kernels, per_device(): pl.pallas_call(kernel, out_shape=(jax.ShapeDtypeStruct((1, FACE), F32), j...  45.9 us

profile of v5, /device:TPU:2, one launch (start us, length us, event | category | flops | bytes accessed | tf_op | source)
XLA Modules:
  0.0 48.1 jit_solution(3545622993243861282)
XLA Ops:
  1.3 45.9 %margin_step.1 = (f32[1,64]{1,0:T(1,128)S(1)}, f32[64,512]{1,0:T(8,128)S(1)}, f32[128,512]{1,0:T(8,128)S(1)}, f32[128,512]{1,0:T(8,128)S(1)}) custom-call(bf16[64,512]{1,0:T(8,128)(2,1)} %faces_ref.1, bf16[512,512]{1,0:T(8,128)(2,1)} %w_first_ref.1, bf16[512,512]{1,0:T(8,128)(2,1)} %w_second_ref.1, f32[1,512]{1,0:T(1,128)} %bitcast.5, f32[1,512]{1,0:T(1,128)} %bitcast.6, ...), custom_call_target="tpu_custom_call" | custom-call | tf_op jit(solution)/shard_map/margin_step/pallas_call | solution.py:450
  47.2 0.9 %hand_over.1 = (f32[1,64]{1,0:T(1,128)}, f32[64,512]{1,0:T(8,128)}, f32[128,512]{1,0:T(8,128)}, f32[128,512]{1,0:T(8,128)}) custom-call(f32[1,64]{1,0:T(1,128)S(1)} %get-tuple-element.12.refs_0_, f32[64,512]{1,0:T(8,128)S(1)} %get-tuple-element.13.refs_1_, f32[128,512]{1,0:T(8,128)S(1)} %get-tuple-element.14.refs_2_, f32[128,512]{1,0:T(8,128)S(1)} %get-tuple-element.15.refs_3_), custom_call_target="tpu_custom_call" | custom-call | tf_op jit(solution)/shard_map/hand_over/pallas_call | solution.py:519
